TPU v7x, 768 devices: a whole 4x8x12 slice. The times are simulated.
768 devices in a mesh: dp: 16 (over x, y_lo), blocks: 48 (over z, y_hi, core).
Axes of the slice: x: 4, y: 8 (y_hi: 2, y_lo: 4; y = y_hi * 4 + y_lo), z: 12, core: 2. Of those that a mesh axis runs over, the one named last changes fastest.
Arguments:
- grads: bfloat16 [16, 336, 512, 512], P('dp', 'blocks'), may hold values from -640 to 640, as said below
- owner: int32 [336, 1], P('blocks'), may hold values from 0 to 15; in each aligned block of 7 rows (0 to 6, 7 to 13, ...) at most 2 rows name the same one
Outputs:
- owned_roots: bfloat16 [48, 16, 2, 512, 512], P('blocks', 'dp')
Inputs may be any that keep to these rules, and one draw needn't show every extreme that they name: `grads`: gradient entries are finite. `owner`: among the 7 blocks of one column (aligned blocks of 7 rows), no dp index is named more than 2 times, and some column names one exactly 2 times.
All inputs are finite; a program needn't handle non-finite values.
Results may differ from a plain program's by a relative error of at most 0.015.
Values may be sent and summed in bfloat16 or wider, within the bound.
A program may use at most 32 MiB of HBM per device.

v0:
```python
import jax
import jax.numpy as jnp
from jax import lax
from jax.sharding import PartitionSpec as P

CAP = 2
ITERS = 2


clip_level = 0.25
ridge = 0.02


def product(left, right):
    return jnp.einsum("nik,nkj->nij", left, right, preferred_element_type=jnp.float32)


def newton(stat_bf):
    order = stat_bf.shape[-1]
    unit = jnp.eye(order, dtype=jnp.float32)
    stat_f = stat_bf.astype(jnp.float32)
    scale_z = (
        0.5 * order**0.5 * lax.rsqrt(jnp.sum(stat_f * stat_f, axis=(1, 2)) + 1e-06)[:, None, None]
    )
    coupled = scale_z * stat_f
    iterate = None
    for step in range(ITERS):
        factor = ((5.0 * unit - coupled) * 0.25).astype(jnp.bfloat16)
        if step == 0:
            iterate = (jnp.sqrt(jnp.sqrt(scale_z)) * factor.astype(jnp.float32)).astype(
                jnp.bfloat16
            )
        else:
            iterate = product(iterate, factor).astype(jnp.bfloat16)
        if step + 1 < ITERS:
            square_t = product(factor, factor).astype(jnp.bfloat16)
            fourth_t = product(square_t, square_t).astype(jnp.bfloat16)
            coupled = product(fourth_t, coupled.astype(jnp.bfloat16))
    return iterate


def newton_items(blocks):
    return newton(blocks[0])[None]


def slot_table(owner_col, replicas):
    count = owner_col.shape[0]
    position = jnp.arange(count, dtype=jnp.int32)
    same = owner_col[:, None] == owner_col[None, :]
    earlier = position[None, :] < position[:, None]
    slot_rank = jnp.sum((same & earlier).astype(jnp.int32), axis=1)
    targets = jnp.arange(replicas, dtype=jnp.int32)
    slots = jnp.arange(CAP, dtype=jnp.int32)
    hit = (owner_col[None, None, :] == targets[:, None, None]) & (
        slot_rank[None, None, :] == slots[None, :, None]
    )
    return hit.astype(jnp.float32)


def body(grads, owner):
    replicas = lax.axis_size("dp")
    my_index = lax.axis_index("dp")
    grad_mat = grads[0]
    blocks_here = grad_mat.shape[0]
    order = grad_mat.shape[1]
    rows = order // replicas
    entries = lax.axis_size("blocks") * blocks_here * order * order
    local_sq = jnp.sum(jnp.square(grad_mat.astype(jnp.float32)))
    total_sq = lax.psum(local_sq, "blocks")
    scale = jnp.minimum(1.0, clip_level * lax.rsqrt(total_sq / entries + 1e-06))
    weight = scale * scale / (replicas * order)
    outer = jnp.einsum("jrc,jkc->rjk", grad_mat, grad_mat, preferred_element_type=jnp.float32)
    summed = lax.psum_scatter(
        (weight * outer).astype(jnp.bfloat16), "dp", scatter_dimension=0, tiled=True
    ).astype(jnp.float32)
    row_ids = my_index * rows + lax.broadcasted_iota(jnp.int32, (rows, order), 0)
    col_ids = lax.broadcasted_iota(jnp.int32, (rows, order), 1)
    diagonal = jnp.where(row_ids == col_ids, ridge, 0.0).astype(jnp.float32)
    stat_rows = (summed + diagonal[:, None, :]).astype(jnp.bfloat16)
    owner_col = owner[:, 0]
    onehot = slot_table(owner_col, replicas)
    owned_count = jnp.sum((owner_col == my_index).astype(jnp.int32))
    live_slot = jnp.arange(CAP, dtype=jnp.int32) < owned_count
    send_buf = jnp.einsum(
        "osj,rjc->osrc", onehot.astype(jnp.bfloat16), stat_rows, preferred_element_type=jnp.float32
    ).astype(jnp.bfloat16)
    roots = newton_items(lax.all_to_all(send_buf, "dp", split_axis=0, concat_axis=2, tiled=True))
    owned = jnp.where(live_slot[None, :, None, None], roots, jnp.zeros_like(roots))
    return owned[None]


def solution(mesh):
    return jax.shard_map(
        body,
        mesh=mesh,
        in_specs=(P("dp", "blocks", None, None), P("blocks", None)),
        out_specs=P("blocks", "dp", None, None, None),
        check_vma=False,
    )
```

profile of v0, /device:TPU:56, one launch (start us, length us, event | category | flops | bytes accessed | tf_op | source)
XLA Modules:
  0.0 317.5 jit_solution(13285367989040848681)
XLA Ops:
  6.5 0.0 reduce-scatter.2.cloned.1.call-start
  6.5 4.5 %multiply_reduce_fusion = f32[]{:T(128)} fusion(bf16[1,7,512,512]{3,2,1,0:T(8,128)(2,1)} %param.2), kind=kLoop, calls=%fused_computation.1 | loop fusion | flops 5505023 | bytes 3670020 | tf_op jit(solution)/shard_map/reduce_sum | solution.py:68
  11.1 135.5 %psum.7 = f32[]{:T(128)} all-reduce(f32[]{:T(128)} %multiply_reduce_fusion), channel_id=1, replica_groups=mesh['dp'=16,'blocks'=48] {'blocks'}, use_global_device_ids=true, to_apply=%region_3.4 | all-reduce | flops 1 | bytes 8 | tf_op jit(solution)/shard_map/psum | solution.py:69
  147.3 7.1 %fusion = bf16[512,7,512]{0,2,1:T(8,128)(2,1)} fusion(f32[]{:T(128)S(6)} %div.7, bf16[1,7,512,512]{3,2,1,0:T(8,128)(2,1)} %param.2), kind=kOutput, calls=%fused_computation.2 | convolution fusion | flops 1882718208 | bytes 7340036 | tf_op jit(solution)/shard_map/jrc,jkc->rjk/dot_general | solution.py:72
  154.4 7.9 %copy.10 = bf16[512,7,512]{2,1,0:T(8,128)(2,1)} copy(bf16[512,7,512]{0,2,1:T(8,128)(2,1)} %fusion) | data formatting | bytes 7340032 | tf_op jit(solution)/shard_map/convert_element_type | solution.py:74
  162.3 0.0 copy-start.1
  162.3 0.0 reduce-scatter.2.cloned.1.call-update
  162.3 0.6 copy-done.1
  163.0 0.2 convert_reduce_fusion
  163.1 0.1 iota_compare_fusion.3
  163.2 0.1 fusion.13
  163.3 102.9 %reduce-scatter.2.cloned.1.call-done = bf16[32,7,512]{2,1,0:T(8,128)(2,1)} async-done(((bf16[512,7,512]{2,1,0:T(8,128)(2,1)}), bf16[32,7,512]{2,1,0:T(8,128)(2,1)}) %reduce-scatter.2.cloned.1.call-update) | async-done | bytes 229392 | tf_op jit(solution)/shard_map/reduce_scatter | solution.py:73
  266.2 1.5 convolution_convert_fusion.3
  267.7 1.5 copy.11
  269.2 7.9 %all-to-all-start = ((bf16[16,2,32,512]{3,2,1,0:T(8,128)(2,1)}), bf16[16,2,32,512]{3,2,1,0:T(8,128)(2,1)S(1)}, u32[]{:S(2)}, u32[]{:S(2)}) async-start(bf16[16,2,32,512]{3,2,1,0:T(8,128)(2,1)} %copy.11), calls=%async_computation.1 | async-start | bytes 2097152 | tf_op jit(solution)/shard_map/all_to_all | solution.py:87
  277.1 0.7 fusion.19
  277.9 0.7 iota_compare_fusion.5
  278.6 0.1 fusion.9
  278.7 21.3 %all-to-all-done = bf16[16,2,32,512]{3,2,1,0:T(8,128)(2,1)S(1)} async-done(((bf16[16,2,32,512]{3,2,1,0:T(8,128)(2,1)}), bf16[16,2,32,512]{3,2,1,0:T(8,128)(2,1)S(1)}, u32[]{:S(2)}, u32[]{:S(2)}) %all-to-all-start) | async-done | bytes 1048608 | tf_op jit(solution)/shard_map/all_to_all | solution.py:87
  300.0 0.4 multiply_reduce_fusion.1
  300.4 1.4 fusion.5
  301.8 0.0 copy-start
  301.8 5.4 %convolution_convert_fusion.1 = bf16[2,512,512]{2,1,0:T(8,128)(2,1)} fusion(bf16[2,512,512]{2,1,0:T(8,128)(2,1)} %get-tuple-element.6), kind=kOutput, calls=%fused_computation.12 | convolution fusion | flops 1074790400 | bytes 2097152 | tf_op jit(solution)/shard_map/nik,nkj->nij/dot_general | solution.py:15
  307.2 0.0 copy-done
  307.2 3.5 %fusion.7 = bf16[1,1,2,512,512]{4,3,2,1,0:T(8,128)(2,1)} fusion(bf16[2,512,512]{2,1,0:T(8,128)(2,1)S(1)} %copy-done, f32[2]{0:T(128)S(1)} %get-tuple-element.7, pred[2]{0:T(512)(128)(4,1)S(1)} %iota_compare_fusion.5, bf16[2,512,512]{2,1,0:T(8,128)(2,1)} %convolution_convert_fusion.1, bf16[2,512,512]{2,1,0:T(8,128)(2,1)S(1)} %get-tuple-element.5, ...), kind=kOutput, calls=%fused_computation.16 | convolution fusion | flops 1077936128 | bytes 5242890 | tf_op jit(solution)/shard_map/nik,nkj->nij/dot_general | solution.py:15
  (3 shorter events, 0.0 us)
Async XLA Ops:
  6.5 259.6 %reduce-scatter.2.cloned.1.call-start = ((), (), s32[]{:S(2)}) async-start(), calls=%async_computation.2 | async-start | bytes 4456448 | tf_op jit(solution)/shard_map/reduce_scatter | solution.py:73
  162.3 0.7 copy-start.1
  269.2 30.7 %all-to-all-start = ((bf16[16,2,32,512]{3,2,1,0:T(8,128)(2,1)}), bf16[16,2,32,512]{3,2,1,0:T(8,128)(2,1)S(1)}, u32[]{:S(2)}, u32[]{:S(2)}) async-start(bf16[16,2,32,512]{3,2,1,0:T(8,128)(2,1)} %copy.11), calls=%async_computation.1 | async-start | bytes 2097152 | tf_op jit(solution)/shard_map/all_to_all | solution.py:87
  301.8 5.4 %copy-start = (bf16[2,512,512]{2,1,0:T(8,128)(2,1)S(1)}, bf16[2,512,512]{2,1,0:T(8,128)(2,1)}, u32[]{:S(2)}) copy-start(bf16[2,512,512]{2,1,0:T(8,128)(2,1)} %get-tuple-element.6) | copy-start | bytes 3145732
Sparse Core Ops, SparseCore 0:
  162.4 103.6 reduce-scatter.1
where the time goes:
time: 320 us; the launch traced here: 318 us
  blocking collectives  136 us (42%)
  waiting for transfers between devices  124 us (39%)
  matrix products  17.5 us (5%)
  between operations  14.1 us (4%)
  local copies, waits for them, and re-layouts  10.1 us (3%)
  other arithmetic  8.23 us (3%)
  starting transfers between devices  7.9 us (2%)
    psum x1, blocking collectives, body(): total_sq = lax.psum(local_sq, 'blocks')  136 us
    reduce_scatter x1, waiting for transfers between devices, body(): lax.psum_scatter((weight * outer).astype(jnp.bfloat16), 'dp', scatter_dim...  103 us
    all_to_all x1, waiting for transfers between devices, body(): lax.all_to_all(send_buf, 'dp', split_axis=0, concat_axis=2, tiled=True)  21.3 us
    dot_general x2, matrix products, product(): jnp.einsum('nik,nkj->nij', left, right, preferred_element_type=jnp.float32)  8.85 us
    convert_element_type x1, local copies, waits for them, and re-layouts, body(): (weight * outer).astype(jnp.bfloat16)  7.9 us
    all_to_all x1, starting transfers between devices, body(): lax.all_to_all(send_buf, 'dp', split_axis=0, concat_axis=2, tiled=True)  7.9 us
    dot_general x1, matrix products, body(): jnp.einsum('jrc,jkc->rjk', grad_mat, grad_mat, preferred_element_type=jnp...  7.09 us
  transfers between devices with their start and end apart: 2, of which 2 were waited for; matrix products, arithmetic and copies ran while one was open for 1% of the time, Pallas kernels for 0%

commit v1 on v0

v1 whole, which is shorter than its diff:
```python
import functools

import jax
import jax.numpy as jnp
from jax import lax
from jax.experimental import pallas as pl
from jax.experimental.pallas import tpu as pltpu
from jax.sharding import PartitionSpec as P

CAP = 2
CLIP = 0.25
RIDGE = 0.02
T = 128
QUARTER = 256
PIECE = 64
NX = 4
NY = 4
NC = 4
MESH = pl.DeviceIdType.MESH
F32 = jnp.float32
BF16 = jnp.bfloat16


def gram(left, right):
    return lax.dot_general(left, right, (((1,), (1,)), ((), ())), preferred_element_type=F32)


def exchange_kernel(
    n_blocks, count, entries,
    owner_ref, grads_ref,
    pieces_out, diag_out,
    g_buf, packed, xr1, xr2, xr3, xs2, xsum, yr, stat, a2a_send, zbuf, cbuf, wbuf, ebuf, eybuf, slot_idx,
    g_sem, x_send, x_recv, y_send, y_recv, a_send, a_recv, z_send, z_recv, c_send, c_recv, w_send, w_recv,
    e_send, e_recv, ey_send, ey_recv, out_sem,
):
    nz = n_blocks // NC
    me = lax.axis_index("dp")
    col = lax.axis_index("blocks")
    x, y = me // NY, me % NY
    z, c = col // NC, col % NC

    def dp_id(xx, yy):
        return {"dp": xx * NY + yy, "blocks": col}

    def col_id(zz, cc):
        return {"dp": me, "blocks": zz * NC + cc}

    right, left = lax.rem(x + 1, NX), lax.rem(x + NX - 1, NX)
    opposite = lax.rem(x + 2, NX)

    def remote(src, dst, ssem, rsem, dev):
        return pltpu.make_async_remote_copy(
            src_ref=src, dst_ref=dst, send_sem=ssem, recv_sem=rsem, device_id=dev, device_id_type=MESH
        )

    def load(j):
        return pltpu.make_async_copy(grads_ref.at[0, j], g_buf.at[j], g_sem.at[j])

    for j in range(count):
        load(j).start()

    barrier = pltpu.get_barrier_semaphore()

    @pl.loop(1, NX * NY)
    def _(k):
        peer = lax.rem(me + k, NX * NY)
        pl.semaphore_signal(barrier, inc=1, device_id={"dp": peer, "blocks": col}, device_id_type=MESH)

    if nz > 1:
        @pl.loop(1, nz)
        def _(k):
            pl.semaphore_signal(barrier, inc=1, device_id=col_id(lax.rem(z + k, nz), c), device_id_type=MESH)

    @pl.loop(1, NC)
    def _(k):
        pl.semaphore_signal(barrier, inc=1, device_id=col_id(z, lax.rem(c + k, NC)), device_id_type=MESH)

    pl.semaphore_wait(barrier, NX * NY - 1 + nz - 1 + NC - 1)

    def x_copy(kind, j):
        half_a, half_b = pl.ds(0, T), pl.ds(T, T)
        src = {
            0: lambda: packed.at[j, opposite, half_a],
            1: lambda: packed.at[j, opposite, half_b],
            2: lambda: packed.at[j, right, half_b],
            3: lambda: packed.at[j, left, half_a],
            4: lambda: xs2.at[0, j],
            5: lambda: xs2.at[1, j],
        }[kind]()
        dst = {0: xr1, 1: xr1, 2: xr3, 3: xr3, 4: xr2, 5: xr2}[kind].at[kind % 2, j]
        to = right if kind % 2 == 0 else left
        return remote(src, dst, x_send.at[kind, j], x_recv.at[kind, j], dp_id(to, y))

    rows = lax.broadcasted_iota(jnp.int32, (T, T), 0)
    cols = lax.broadcasted_iota(jnp.int32, (T, T), 1)
    lower = rows >= cols
    eye = rows == cols

    zbuf[z] = jnp.zeros((8, T), F32)
    ebuf[x] = jnp.zeros((16, T), F32)

    @pl.loop(0, count)
    def _(j):
        load(j).wait()
        top, bottom = g_buf[j, :256], g_buf[j, 256:]
        cross = gram(bottom, top)
        for t, (r, k) in enumerate(((0, 0), (0, 1), (1, 0), (1, 1))):
            packed[j, t // 2, (t % 2) * T:(t % 2 + 1) * T, :] = cross[
                r * T:(r + 1) * T, k * T:(k + 1) * T
            ].astype(BF16)
        square = jnp.zeros((T, T), F32)
        for h, part in enumerate((top, bottom)):
            own = gram(part, part)
            d0, d1 = own[:T, :T], own[T:, T:]
            packed[j, 2, h * T:(h + 1) * T, :] = own[T:, :T].astype(BF16)
            packed[j, 3, h * T:(h + 1) * T, :] = jnp.where(lower, d0, d1).astype(BF16)
            e1 = jnp.where(eye, d1, 0.0)
            ebuf[x, pl.ds(2 * j + h, 1), :] = jnp.sum(e1, axis=0, keepdims=True)
            square = square + jnp.where(eye, d0, 0.0) + e1
        zbuf[z] += jnp.sum(square.reshape(T // 8, 8, T), axis=0)
        x_copy(0, j).start()
        x_copy(1, j).start()

    def z_copy(k, incoming):
        peer = lax.rem(z + k, nz)
        at = peer if incoming else z
        return remote(zbuf.at[at], zbuf.at[at], z_send.at[k], z_recv.at[at], col_id(peer, c))

    def c_copy(k, incoming):
        peer = lax.rem(c + k, NC)
        at = peer if incoming else c
        return remote(cbuf.at[at], cbuf.at[at], c_send.at[k], c_recv.at[at], col_id(z, peer))

    def w_copy(k, incoming):
        peer = lax.rem(x + k, NX)
        at = peer if incoming else x
        return remote(wbuf.at[at], wbuf.at[at], w_send.at[k], w_recv.at[at], dp_id(peer, y))

    def e_copy(k, incoming):
        peer = lax.rem(x + k, NX)
        at = peer if incoming else x
        return remote(ebuf.at[at], ebuf.at[at], e_send.at[k], e_recv.at[at], dp_id(peer, y))

    def ey_copy(k, incoming):
        peer = lax.rem(y + k, NY)
        at = peer if incoming else y
        return remote(eybuf.at[at], eybuf.at[at], ey_send.at[k], ey_recv.at[at], dp_id(x, peer))

    if nz > 1:
        @pl.loop(1, nz)
        def _(k):
            z_copy(k, False).start()

    @pl.loop(1, NX)
    def _(k):
        e_copy(k, False).start()

    @pl.loop(0, count)
    def _(j):
        x_copy(2, j).start()
        x_copy(3, j).start()

    @pl.loop(0, NX * NY * CAP)
    def _(i):
        target, slot = i // CAP, i % CAP
        found = jnp.int32(count)
        seen = jnp.int32(0)
        for j in range(count):
            hit = owner_ref[j, 0] == target
            found = jnp.where(jnp.logical_and(hit, seen == slot), j, found)
            seen = seen + jnp.where(hit, 1, 0)
        slot_idx[i] = found

    stat[count] = jnp.zeros((PIECE, T), BF16)

    if nz > 1:
        @pl.loop(1, nz)
        def _(k):
            z_copy(k, True).wait_recv()

    cbuf[c] = jnp.sum(zbuf[...], axis=0)

    @pl.loop(1, NC)
    def _(k):
        c_copy(k, False).start()

    @pl.loop(1, NC)
    def _(k):
        c_copy(k, True).wait_recv()

    total = jnp.sum(jnp.sum(cbuf[...], axis=0), axis=(0, 1), keepdims=True)
    scale = jnp.minimum(1.0, CLIP * lax.rsqrt(jnp.broadcast_to(total, (8, T)) / entries + 1e-06))
    wbuf[x] = scale * scale / (NX * NY * 512)

    @pl.loop(1, NX)
    def _(k):
        w_copy(k, False).start()

    @pl.loop(1, NX)
    def _(k):
        w_copy(k, True).wait_recv()

    w_me, w_left, w_right = wbuf[x, 0:1, :], wbuf[left, 0:1, :], wbuf[right, 0:1, :]

    def wide(value):
        return value.astype(F32)

    @pl.loop(0, count)
    def _(j):
        x_copy(0, j).wait_recv()
        xs2[0, j] = (w_left * wide(xr1[0, j]) + w_me * wide(packed[j, right, :T, :])).astype(BF16)
        x_copy(4, j).start()
        x_copy(1, j).wait_recv()
        xs2[1, j] = (w_right * wide(xr1[1, j]) + w_me * wide(packed[j, left, T:, :])).astype(BF16)
        x_copy(5, j).start()

    @pl.loop(1, NX)
    def _(k):
        e_copy(k, True).wait_recv()

    diag = jnp.zeros((16, T), F32)
    for k in range(NX):
        diag = diag + wbuf[k, 0:1, :] * ebuf[k]
    eybuf[y] = diag

    @pl.loop(1, NY)
    def _(k):
        ey_copy(k, False).start()

    def y_copy(k, j, incoming):
        peer = lax.rem(y + k, NY)
        at = peer if incoming else y
        piece = pl.ds(pl.multiple_of(peer * PIECE, PIECE), PIECE)
        return remote(xsum.at[j, piece], yr.at[j, at], y_send.at[k, j], y_recv.at[j, at], dp_id(x, peer))

    @pl.loop(0, count)
    def _(j):
        for kind in (2, 3, 4, 5):
            x_copy(kind, j).wait_recv()
        half_a = w_me * wide(packed[j, x, :T, :]) + wide(xr2[0, j]) + w_right * wide(xr3[1, j])
        half_b = w_me * wide(packed[j, x, T:, :]) + wide(xr2[1, j]) + w_left * wide(xr3[0, j])
        xsum[j, :T, :] = half_a.astype(BF16)
        xsum[j, T:, :] = half_b.astype(BF16)
        yr[j, y] = xsum[j, pl.ds(pl.multiple_of(y * PIECE, PIECE), PIECE), :]
        for k in range(1, NY):
            y_copy(k, j, False).start()

    packed_row = me * PIECE + lax.broadcasted_iota(jnp.int32, (PIECE, T), 0)
    on_diagonal = jnp.logical_and(packed_row >= 6 * T, packed_row % T == lax.broadcasted_iota(jnp.int32, (PIECE, T), 1))
    ridge = jnp.where(on_diagonal, RIDGE, 0.0).astype(F32)

    @pl.loop(0, count)
    def _(j):
        for k in range(1, NY):
            y_copy(k, j, True).wait_recv()
        got = wide(yr[j, 0]) + wide(yr[j, 1]) + wide(yr[j, 2]) + wide(yr[j, 3])
        stat[j] = (got + ridge).astype(BF16)

    @pl.loop(0, NX * NY)
    def _(o):
        for s in range(CAP):
            a2a_send[o, s] = stat[slot_idx[o * CAP + s]]

    def a_copy(k, incoming):
        peer = lax.rem(me + k, NX * NY)
        at = peer if incoming else me
        return remote(a2a_send.at[peer], pieces_out.at[at], a_send.at[k], a_recv.at[at], {"dp": peer, "blocks": col})

    @pl.loop(1, NX * NY)
    def _(k):
        a_copy(k, False).start()

    mine = pltpu.make_async_copy(a2a_send.at[me], pieces_out.at[me], out_sem)
    mine.start()

    @pl.loop(1, NY)
    def _(k):
        ey_copy(k, True).wait_recv()

    diag_out[...] = eybuf[0] + eybuf[1] + eybuf[2] + eybuf[3]

    if nz > 1:
        @pl.loop(1, nz)
        def _(k):
            z_copy(k, False).wait_send()

    @pl.loop(1, NX)
    def _(k):
        c_copy(k, False).wait_send()
        w_copy(k, False).wait_send()
        e_copy(k, False).wait_send()
        ey_copy(k, False).wait_send()

    @pl.loop(0, count)
    def _(j):
        for kind in range(6):
            x_copy(kind, j).wait_send()
        for k in range(1, NY):
            y_copy(k, j, False).wait_send()

    @pl.loop(1, NX * NY)
    def _(k):
        a_copy(k, True).wait_recv()
        a_copy(k, False).wait_send()

    mine.wait()


def product(left, right):
    return lax.dot_general(left, right, (((1,), (0,)), ((), ())), preferred_element_type=F32)


def newton_kernel(count, owner_ref, index_ref, pieces_ref, diag_ref, out_ref, mat):
    order = mat.shape[-1]
    me = index_ref[0]
    rows = lax.broadcasted_iota(jnp.int32, (T, T), 0)
    cols = lax.broadcasted_iota(jnp.int32, (T, T), 1)
    unit5 = jnp.where(
        lax.broadcasted_iota(jnp.int32, (order, order), 0) == lax.broadcasted_iota(jnp.int32, (order, order), 1), 5.0, 0.0
    ).astype(F32)
    for s in range(CAP):
        found = jnp.int32(0)
        seen = jnp.int32(0)
        for j in range(count):
            hit = owner_ref[j, 0] == me
            found = jnp.where(jnp.logical_and(hit, seen == s), j, found)
            seen = seen + jnp.where(hit, 1, 0)
        live = seen > s

        def tile(t):
            return jnp.concatenate([pieces_ref[2 * t, s], pieces_ref[2 * t + 1, s]], axis=0).astype(F32)

        def put(r, k, value):
            mat[s, r * T:(r + 1) * T, k * T:(k + 1) * T] = value

        for t, (r, k) in enumerate(((2, 0), (2, 1), (3, 0), (3, 1), (1, 0), (3, 2))):
            value = tile(t)
            put(r, k, value)
            put(k, r, value.T)
        for h in range(2):
            value = tile(6 + h)
            turned = value.T
            edge = (diag_ref[pl.ds(2 * found + h, 1), :] + RIDGE).astype(BF16).astype(F32)
            put(2 * h, 2 * h, jnp.where(rows >= cols, value, turned))
            put(2 * h + 1, 2 * h + 1, jnp.where(rows < cols, value, jnp.where(rows == cols, edge, turned)))
        full = mat[s]
        z = 0.5 * order**0.5 * lax.rsqrt(jnp.sum(full * full, axis=(0, 1), keepdims=True) + 1e-06)
        coupled = z * full
        factor = ((unit5 - coupled) * 0.25).astype(BF16)
        iterate = (jnp.sqrt(jnp.sqrt(z)) * factor.astype(F32)).astype(BF16)
        square = product(factor, factor).astype(BF16)
        fourth = product(square, square).astype(BF16)
        coupled = product(fourth, coupled.astype(BF16))
        factor = ((unit5 - coupled) * 0.25).astype(BF16)
        root = product(iterate, factor)
        out_ref[s] = jnp.where(live, root, 0.0).astype(BF16)


def body(n_blocks, grads, owner):
    count, order = grads.shape[1], grads.shape[2]
    entries = n_blocks * count * order * order
    n = NX * NY
    nz = n_blocks // NC
    dma = pltpu.SemaphoreType.DMA
    vmem = pltpu.VMEM
    pieces, diag = pl.pallas_call(
        functools.partial(exchange_kernel, n_blocks, count, float(entries)),
        out_shape=(
            jax.ShapeDtypeStruct((n, CAP, PIECE, T), BF16),
            jax.ShapeDtypeStruct((16, T), F32),
        ),
        in_specs=[pl.BlockSpec(memory_space=pltpu.SMEM), pl.BlockSpec(memory_space=pl.ANY)],
        out_specs=(pl.BlockSpec(memory_space=pl.ANY), pl.BlockSpec(memory_space=pltpu.VMEM)),
        scratch_shapes=[
            vmem((count, order, order), BF16),
            vmem((count, NX, QUARTER, T), BF16),
            vmem((2, count, T, T), BF16),
            vmem((2, count, T, T), BF16),
            vmem((2, count, T, T), BF16),
            vmem((2, count, T, T), BF16),
            vmem((count, QUARTER, T), BF16),
            vmem((count, NY, PIECE, T), BF16),
            vmem((count + 1, PIECE, T), BF16),
            vmem((n, CAP, PIECE, T), BF16),
            vmem((nz, 8, T), F32),
            vmem((NC, 8, T), F32),
            vmem((NX, 8, T), F32),
            vmem((NX, 16, T), F32),
            vmem((NY, 16, T), F32),
            pltpu.SMEM((n * CAP,), jnp.int32),
            dma((count,)),
            dma((6, count)), dma((6, count)),
            dma((NY, count)), dma((count, NY)),
            dma((n,)), dma((n,)),
            dma((nz,)), dma((nz,)),
            dma((NC,)), dma((NC,)),
            dma((NX,)), dma((NX,)),
            dma((NX,)), dma((NX,)),
            dma((NY,)), dma((NY,)),
            dma(()),
        ],
        compiler_params=pltpu.CompilerParams(
            collective_id=0, has_side_effects=True, vmem_limit_bytes=32 * 1024 * 1024
        ),
        cost_estimate=pl.CostEstimate(flops=2 * count * order**3, bytes_accessed=grads.size * 2, transcendentals=0),
        name="exchange",
    )(owner, grads)
    index = lax.axis_index("dp").reshape(1).astype(jnp.int32)
    roots = pl.pallas_call(
        functools.partial(newton_kernel, count),
        out_shape=jax.ShapeDtypeStruct((CAP, order, order), BF16),
        in_specs=[
            pl.BlockSpec(memory_space=pltpu.SMEM),
            pl.BlockSpec(memory_space=pltpu.SMEM),
            pl.BlockSpec(memory_space=pltpu.VMEM),
            pl.BlockSpec(memory_space=pltpu.VMEM),
        ],
        out_specs=pl.BlockSpec(memory_space=pltpu.VMEM),
        scratch_shapes=[vmem((CAP, order, order), F32)],
        compiler_params=pltpu.CompilerParams(vmem_limit_bytes=32 * 1024 * 1024),
        cost_estimate=pl.CostEstimate(flops=16 * order**3, bytes_accessed=4 * order * order, transcendentals=0),
        name="newton",
    )(owner, index, pieces, diag)
    return roots[None, None]


def solution(mesh):
    return jax.shard_map(
        functools.partial(body, mesh.shape["blocks"]),
        mesh=mesh,
        in_specs=(P("dp", "blocks", None, None), P("blocks", None)),
        out_specs=P("blocks", "dp", None, None, None),
        check_vma=False,
    )
```

time: 320 us -> 72.2 us (0.23)
  the two profiles are of different devices: /device:TPU:56 before, /device:TPU:2 now
where the time goes in v1:
time: 72.2 us; the launch traced here: 72 us
  Pallas kernels  69.2 us (96%)
  local copies, waits for them, and re-layouts  2.78 us (4%)
    pallas_call x1, Pallas kernels, body(): pl.pallas_call(functools.partial(exchange_kernel, n_blocks, count, float(...  64.4 us
    pallas_call x1, Pallas kernels, body(): pl.pallas_call(functools.partial(newton_kernel, count), out_shape=jax.Sha...  4.85 us
    unnamed x3, local copies, waits for them, and re-layouts  2.78 us

profile of v1, /device:TPU:2, one launch (start us, length us, event | category | flops | bytes accessed | tf_op | source)
XLA Modules:
  0.0 72.0 jit_solution(15448690259693020921)
XLA Ops:
  0.0 0.7 %copy.4.owner_ref = s32[7,1]{1,0:T(8,128)S(1)} copy(s32[7,1]{0,1:T(1,128)} %param.3) | data formatting | bytes 56 | tf_op args[1]
  0.7 0.0 copy-start
  0.7 2.0 %copy-done = bf16[1,7,512,512]{3,2,1,0:T(8,128)(2,1)S(1)} copy-done((bf16[1,7,512,512]{3,2,1,0:T(8,128)(2,1)S(1)}, bf16[1,7,512,512]{3,2,1,0:T(8,128)(2,1)}, u32[]{:S(2)}) %copy-start) | copy-done | bytes 3670040
  2.8 64.4 %exchange.1 = (bf16[16,2,64,128]{3,2,1,0:T(8,128)(2,1)S(1)}, f32[16,128]{1,0:T(8,128)S(1)}) custom-call(s32[7,1]{1,0:T(8,128)S(1)} %copy.4.owner_ref, bf16[1,7,512,512]{3,2,1,0:T(8,128)(2,1)S(1)} %copy-done), custom_call_target="tpu_custom_call" | custom-call | flops 1879048192 | bytes 3670016 | tf_op jit(solution)/shard_map/exchange/pallas_call | solution.py:366
  67.1 4.8 %newton.1 = bf16[2,512,512]{2,1,0:T(8,128)(2,1)} custom-call(s32[7,1]{1,0:T(8,128)S(1)} %copy.4.owner_ref, s32[1]{0:T(128)} %bitcast.index_ref, bf16[16,2,64,128]{3,2,1,0:T(8,128)(2,1)S(1)} %get-tuple-element.7.pieces_ref, f32[16,128]{1,0:T(8,128)S(1)} %get-tuple-element.8.diag_ref), custom_call_target="tpu_custom_call" | custom-call | flops 2147483648 | bytes 1048576 | tf_op jit(solution)/shard_map/newton/pallas_call | solution.py:409
Async XLA Ops:
  0.7 2.0 %copy-start = (bf16[1,7,512,512]{3,2,1,0:T(8,128)(2,1)S(1)}, bf16[1,7,512,512]{3,2,1,0:T(8,128)(2,1)}, u32[]{:S(2)}) copy-start(bf16[1,7,512,512]{3,2,1,0:T(8,128)(2,1)} %grads_ref.1) | copy-start | bytes 11010052

commit v2 on v1

v2 whole, which is shorter than its diff:
```python
import functools

import jax
import jax.numpy as jnp
from jax import lax
from jax.experimental import pallas as pl
from jax.experimental.pallas import tpu as pltpu
from jax.sharding import PartitionSpec as P

CAP = 2
CLIP = 0.25
RIDGE = 0.02
T = 128
QUARTER = 256
PIECE = 64
NX = 4
NY = 4
NC = 4
X_FIRST = 5
MESH = pl.DeviceIdType.MESH
F32 = jnp.float32
BF16 = jnp.bfloat16


def gram(left, right):
    return lax.dot_general(left, right, (((1,), (1,)), ((), ())), preferred_element_type=F32)


def exchange_kernel(
    n_blocks, count, entries,
    owner_ref, grads_ref,
    pieces_out, diag_out,
    g_buf, packed, first_x, first_y, sum_x, sum_y, second_x, second_y, stat, a2a_send,
    zbuf, cbuf, wbuf, ebuf, eybuf, slot_idx,
    g_sem, sems,
):
    nz = n_blocks // NC
    order = g_buf.shape[-1]
    n_x, n_y = min(X_FIRST, count), count - min(X_FIRST, count)
    me = lax.axis_index("dp")
    col = lax.axis_index("blocks")
    x, y = me // NY, me % NY
    z, c = col // NC, col % NC

    def device(xx, yy, zz, cc):
        return {"dp": xx * NY + yy, "blocks": zz * NC + cc}

    def x_peer(k):
        return lax.rem(x + k, NX)

    def y_peer(k):
        return lax.rem(y + k, NY)

    def c_peer(k):
        return lax.rem(c + k, NC)

    Z, C, X1, Y1, X2, Y2, E1, E2, A2A, OWN = range(10)

    def send(group, src, dst, dev):
        pltpu.make_async_remote_copy(
            src_ref=src, dst_ref=dst, send_sem=sems.at[0, group], recv_sem=sems.at[1, group],
            device_id=dev, device_id_type=MESH,
        ).start()

    def whole(group, like):
        return pltpu.make_async_remote_copy(
            src_ref=like, dst_ref=like, send_sem=sems.at[0, group], recv_sem=sems.at[1, group],
            device_id=device(x_peer(1), y, z, c), device_id_type=MESH,
        )

    def load(j):
        return pltpu.make_async_copy(grads_ref.at[0, j], g_buf.at[j], g_sem.at[j])

    barrier = pltpu.get_barrier_semaphore()

    def greet(dev):
        pl.semaphore_signal(barrier, inc=1, device_id=dev, device_id_type=MESH)

    def z_peers(act):
        if nz > 1:
            @pl.loop(1, nz)
            def _(k):
                act(lax.rem(z + k, nz))

    def plane_peers(act):
        @pl.loop(1, NX * NY)
        def _(k):
            act(lax.rem(me + k, NX * NY))

    def weight_peers(act, own_c):
        @pl.loop(0 if own_c else 1, NC)
        def _(k):
            @pl.loop(1, NX)
            def _(i):
                act(device(x_peer(i), y, z, c_peer(k)), 0)
                act(device(x, y_peer(i), z, c_peer(k)), 1)

        @pl.loop(1, NC)
        def _(k):
            act(device(x, y, z, c_peer(k)), 0)

    z_peers(lambda p: greet(device(x, y, p, c)))
    weight_peers(lambda dev, axis: greet(dev), False)
    plane_peers(lambda p: greet({"dp": p, "blocks": col}))
    for j in range(count):
        load(j).start()

    rows = lax.broadcasted_iota(jnp.int32, (T, T), 0)
    cols = lax.broadcasted_iota(jnp.int32, (T, T), 1)
    lower = rows >= cols
    eye = rows == cols
    zbuf[z] = jnp.zeros((8, T), F32)
    ebuf[x] = jnp.zeros((16, T), F32)

    @pl.loop(0, count)
    def _(j):
        load(j).wait()
        top, bottom = g_buf[j, :256], g_buf[j, 256:]
        square = jnp.zeros((T, T), F32)
        for h, part in enumerate((top, bottom)):
            own = gram(part, part)
            d0, d1 = own[:T, :T], own[T:, T:]
            packed[j, 2, h * T:(h + 1) * T, :] = own[T:, :T].astype(BF16)
            packed[j, 3, h * T:(h + 1) * T, :] = jnp.where(lower, d0, d1).astype(BF16)
            e1 = jnp.where(eye, d1, 0.0)
            ebuf[x, pl.ds(2 * j + h, 1), :] = jnp.sum(e1, axis=0, keepdims=True)
            square = square + jnp.where(eye, d0, 0.0) + e1
        zbuf[z] += jnp.sum(square.reshape(T // 8, 8, T), axis=0)
        cross = gram(bottom, top)
        for t, (r, k) in enumerate(((0, 0), (0, 1), (1, 0), (1, 1))):
            packed[j, t // 2, (t % 2) * T:(t % 2 + 1) * T, :] = cross[
                r * T:(r + 1) * T, k * T:(k + 1) * T
            ].astype(BF16)

    pl.semaphore_wait(barrier, NX * NY - 1 + nz - 1 + (NX + NY - 1) * (NC - 1))

    z_peers(lambda p: send(Z, zbuf.at[z], zbuf.at[z], device(x, y, p, c)))

    @pl.loop(0, n_x)
    def _(j):
        @pl.loop(1, NX)
        def _(k):
            to = x_peer(k)
            send(X1, packed.at[j, to], first_x.at[x, j], device(to, y, z, c))

    if n_y:
        @pl.loop(0, n_y)
        def _(j):
            @pl.loop(1, NY)
            def _(k):
                to = y_peer(k)
                send(Y1, packed.at[n_x + j, to], first_y.at[y, j], device(x, to, z, c))

    @pl.loop(1, NX)
    def _(k):
        send(E1, ebuf.at[x], ebuf.at[x], device(x_peer(k), y, z, c))

    @pl.loop(0, NX * NY * CAP)
    def _(i):
        target, slot = i // CAP, i % CAP
        found = jnp.int32(count)
        seen = jnp.int32(0)
        for j in range(count):
            hit = owner_ref[j] == target
            found = jnp.where(jnp.logical_and(hit, seen == slot), j, found)
            seen = seen + jnp.where(hit, 1, 0)
        slot_idx[i] = found

    stat[count] = jnp.zeros((PIECE, T), BF16)

    if nz > 1:
        whole(Z, zbuf.at[pl.ds(0, nz - 1)]).wait_recv()
    total = jnp.sum(zbuf[...], axis=0)
    cbuf[x * NC + c] = total
    cbuf[(NX + y) * NC + c] = total

    def send_sum(dev, axis):
        mine = x if axis == 0 else NX + y
        send(C, cbuf.at[x * NC + c], cbuf.at[mine * NC + c], dev)

    weight_peers(send_sum, True)
    c_like = cbuf.at[pl.ds(0, NX * NC - 1 + (NY - 1) * NC)]
    whole(C, c_like).wait_recv()

    along_x = [jnp.sum(jnp.sum(cbuf[k * NC:(k + 1) * NC], axis=0), axis=0, keepdims=True) for k in range(NX)]
    along_y = [jnp.sum(jnp.sum(cbuf[(NX + k) * NC:(NX + k + 1) * NC], axis=0), axis=0, keepdims=True) for k in range(NY)]
    sums = jnp.sum(jnp.concatenate(along_x + along_y, axis=0), axis=1, keepdims=True)
    scale = jnp.minimum(1.0, CLIP * lax.rsqrt(jnp.broadcast_to(sums, (NX + NY, T)) / entries + 1e-06))
    wbuf[...] = scale * scale / (NX * NY * order)

    def weight_x(k):
        return wbuf[pl.ds(k, 1), :]

    def weight_y(k):
        return wbuf[pl.ds(NX + k, 1), :]

    def wide(value):
        return value.astype(F32)

    whole(X1, first_x.at[pl.ds(0, NX - 1)]).wait_recv()

    @pl.loop(0, n_x)
    def _(j):
        got = weight_x(x) * wide(packed[j, x])
        for k in range(1, NX):
            got = got + weight_x(x_peer(k)) * wide(first_x[x_peer(k), j])
        sum_x[j] = got.astype(BF16)
        for k in range(1, NY):
            to = y_peer(k)
            piece = pl.ds(pl.multiple_of(to * PIECE, PIECE), PIECE)
            send(X2, sum_x.at[j, piece], second_x.at[y, j], device(x, to, z, c))

    if n_y:
        whole(Y1, first_y.at[pl.ds(0, NY - 1)]).wait_recv()

        @pl.loop(0, n_y)
        def _(j):
            got = weight_x(x) * wide(packed[n_x + j, y])
            for k in range(1, NY):
                got = got + weight_y(y_peer(k)) * wide(first_y[y_peer(k), j])
            sum_y[j] = got.astype(BF16)
            for k in range(1, NX):
                to = x_peer(k)
                piece = pl.ds(pl.multiple_of(to * PIECE, PIECE), PIECE)
                send(Y2, sum_y.at[j, piece], second_y.at[x, j], device(to, y, z, c))

    whole(E1, ebuf.at[pl.ds(0, NX - 1)]).wait_recv()
    diag = jnp.zeros((16, T), F32)
    for k in range(NX):
        diag = diag + wbuf[k:k + 1, :] * ebuf[k]
    eybuf[y] = diag

    @pl.loop(1, NY)
    def _(k):
        send(E2, eybuf.at[y], eybuf.at[y], device(x, y_peer(k), z, c))

    lane = lax.broadcasted_iota(jnp.int32, (PIECE, T), 1)
    row = lax.broadcasted_iota(jnp.int32, (PIECE, T), 0)

    def ridge(position):
        packed_row = position * PIECE + row
        on_diagonal = jnp.logical_and(packed_row >= 6 * T, packed_row % T == lane)
        return jnp.where(on_diagonal, RIDGE, 0.0).astype(F32)

    if n_y:
        whole(Y2, second_y.at[pl.ds(0, NX - 1)]).wait_recv()
        ridge_y = ridge(y * NX + x)

        @pl.loop(0, n_y)
        def _(j):
            got = wide(sum_y[j, pl.ds(pl.multiple_of(x * PIECE, PIECE), PIECE), :])
            for k in range(1, NX):
                got = got + wide(second_y[x_peer(k), j])
            stat[n_x + j] = (got + ridge_y).astype(BF16)

    whole(X2, second_x.at[pl.ds(0, NY - 1)]).wait_recv()
    ridge_x = ridge(x * NY + y)

    @pl.loop(0, n_x)
    def _(j):
        got = wide(sum_x[j, pl.ds(pl.multiple_of(y * PIECE, PIECE), PIECE), :])
        for k in range(1, NY):
            got = got + wide(second_x[y_peer(k), j])
        stat[j] = (got + ridge_x).astype(BF16)

    @pl.loop(0, NX * NY)
    def _(k):
        o = lax.rem(me + k, NX * NY)
        for s in range(CAP):
            a2a_send[o, s] = stat[slot_idx[o * CAP + s]]

        @pl.when(k > 0)
        def _():
            send(A2A, a2a_send.at[o], pieces_out.at[me], {"dp": o, "blocks": col})

    mine = pltpu.make_async_copy(a2a_send.at[me], pieces_out.at[me], sems.at[0, OWN])
    mine.start()

    whole(E2, eybuf.at[pl.ds(0, NY - 1)]).wait_recv()
    diag_out[...] = eybuf[0] + eybuf[1] + eybuf[2] + eybuf[3]

    if nz > 1:
        whole(Z, zbuf.at[pl.ds(0, nz - 1)]).wait_send()
    whole(C, c_like).wait_send()
    whole(X1, first_x.at[pl.ds(0, NX - 1)]).wait_send()
    whole(X2, second_x.at[pl.ds(0, NY - 1)]).wait_send()
    if n_y:
        whole(Y1, first_y.at[pl.ds(0, NY - 1)]).wait_send()
        whole(Y2, second_y.at[pl.ds(0, NX - 1)]).wait_send()
    whole(E1, ebuf.at[pl.ds(0, NX - 1)]).wait_send()
    whole(E2, eybuf.at[pl.ds(0, NY - 1)]).wait_send()
    whole(A2A, a2a_send.at[pl.ds(0, NX * NY - 1)]).wait_recv()
    whole(A2A, a2a_send.at[pl.ds(0, NX * NY - 1)]).wait_send()
    mine.wait()


def product(left, right):
    return lax.dot_general(left, right, (((1,), (0,)), ((), ())), preferred_element_type=F32)


def newton_kernel(count, owner_ref, index_ref, pieces_ref, diag_ref, out_ref, mat):
    order = mat.shape[-1]
    me = index_ref[0]
    rows = lax.broadcasted_iota(jnp.int32, (T, T), 0)
    cols = lax.broadcasted_iota(jnp.int32, (T, T), 1)
    unit5 = jnp.where(
        lax.broadcasted_iota(jnp.int32, (order, order), 0) == lax.broadcasted_iota(jnp.int32, (order, order), 1), 5.0, 0.0
    ).astype(F32)
    for s in range(CAP):
        found = jnp.int32(0)
        seen = jnp.int32(0)
        for j in range(count):
            hit = owner_ref[j] == me
            found = jnp.where(jnp.logical_and(hit, seen == s), j, found)
            seen = seen + jnp.where(hit, 1, 0)
        live = seen > s

        x_first = found < X_FIRST

        def tile(t):
            halves = []
            for p in (2 * t, 2 * t + 1):
                halves.append(pieces_ref[jnp.where(x_first, p, p % NX * NY + p // NX), s])
            return jnp.concatenate(halves, axis=0).astype(F32)

        def put(r, k, value):
            mat[s, r * T:(r + 1) * T, k * T:(k + 1) * T] = value

        for t, (r, k) in enumerate(((2, 0), (2, 1), (3, 0), (3, 1), (1, 0), (3, 2))):
            value = tile(t)
            put(r, k, value)
            put(k, r, value.T)
        for h in range(2):
            value = tile(6 + h)
            turned = value.T
            edge = (diag_ref[pl.ds(2 * found + h, 1), :] + RIDGE).astype(BF16).astype(F32)
            put(2 * h, 2 * h, jnp.where(rows >= cols, value, turned))
            put(2 * h + 1, 2 * h + 1, jnp.where(rows < cols, value, jnp.where(rows == cols, edge, turned)))
        full = mat[s]
        z = 0.5 * order**0.5 * lax.rsqrt(jnp.sum(full * full, axis=(0, 1), keepdims=True) + 1e-06)
        coupled = z * full
        factor = ((unit5 - coupled) * 0.25).astype(BF16)
        iterate = (jnp.sqrt(jnp.sqrt(z)) * factor.astype(F32)).astype(BF16)
        square = product(factor, factor).astype(BF16)
        fourth = product(square, square).astype(BF16)
        coupled = product(fourth, coupled.astype(BF16))
        factor = ((unit5 - coupled) * 0.25).astype(BF16)
        root = product(iterate, factor)
        out_ref[s] = jnp.where(live, root, 0.0).astype(BF16)


def body(n_blocks, grads, owner):
    count, order = grads.shape[1], grads.shape[2]
    entries = n_blocks * count * order * order
    n = NX * NY
    n_x = min(X_FIRST, count)
    n_y = max(count - n_x, 1)
    nz = n_blocks // NC
    dma = pltpu.SemaphoreType.DMA
    vmem = pltpu.VMEM
    pieces, diag = pl.pallas_call(
        functools.partial(exchange_kernel, n_blocks, count, float(entries)),
        out_shape=(
            jax.ShapeDtypeStruct((n, CAP, PIECE, T), BF16),
            jax.ShapeDtypeStruct((16, T), F32),
        ),
        in_specs=[pl.BlockSpec(memory_space=pltpu.SMEM), pl.BlockSpec(memory_space=pl.ANY)],
        out_specs=(pl.BlockSpec(memory_space=pl.ANY), pl.BlockSpec(memory_space=pltpu.VMEM)),
        scratch_shapes=[
            vmem((count, order, order), BF16),
            vmem((count, NX, QUARTER, T), BF16),
            vmem((NX, n_x, QUARTER, T), BF16),
            vmem((NY, n_y, QUARTER, T), BF16),
            vmem((n_x, QUARTER, T), BF16),
            vmem((n_y, QUARTER, T), BF16),
            vmem((NY, n_x, PIECE, T), BF16),
            vmem((NX, n_y, PIECE, T), BF16),
            vmem((count + 1, PIECE, T), BF16),
            vmem((n, CAP, PIECE, T), BF16),
            vmem((nz, 8, T), F32),
            vmem(((NX + NY) * NC, 8, T), F32),
            vmem((NX + NY, T), F32),
            vmem((NX, 16, T), F32),
            vmem((NY, 16, T), F32),
            pltpu.SMEM((n * CAP,), jnp.int32),
            dma((count,)),
            dma((2, 10)),
        ],
        compiler_params=pltpu.CompilerParams(
            collective_id=0, has_side_effects=True, vmem_limit_bytes=61 * 1024 * 1024
        ),
        cost_estimate=pl.CostEstimate(flops=2 * count * order**3, bytes_accessed=grads.size * 2, transcendentals=0),
        name="exchange",
    )(owner[:, 0], grads)
    index = lax.axis_index("dp").reshape(1).astype(jnp.int32)
    roots = pl.pallas_call(
        functools.partial(newton_kernel, count),
        out_shape=jax.ShapeDtypeStruct((CAP, order, order), BF16),
        in_specs=[
            pl.BlockSpec(memory_space=pltpu.SMEM),
            pl.BlockSpec(memory_space=pltpu.SMEM),
            pl.BlockSpec(memory_space=pltpu.VMEM),
            pl.BlockSpec(memory_space=pltpu.VMEM),
        ],
        out_specs=pl.BlockSpec(memory_space=pltpu.VMEM),
        scratch_shapes=[vmem((CAP, order, order), F32)],
        compiler_params=pltpu.CompilerParams(vmem_limit_bytes=32 * 1024 * 1024),
        cost_estimate=pl.CostEstimate(flops=16 * order**3, bytes_accessed=4 * order * order, transcendentals=0),
        name="newton",
    )(owner[:, 0], index, pieces, diag)
    return roots[None, None]


def solution(mesh):
    return jax.shard_map(
        functools.partial(body, mesh.shape["blocks"]),
        mesh=mesh,
        in_specs=(P("dp", "blocks", None, None), P("blocks", None)),
        out_specs=P("blocks", "dp", None, None, None),
        check_vma=False,
    )
```

time: 72.2 us -> 64.8 us (0.90)
  the two profiles are of different devices: /device:TPU:2 before, /device:TPU:56 now
where the time goes in v2:
time: 64.8 us; the launch traced here: 64.6 us
  Pallas kernels  62.8 us (97%)
  local copies, waits for them, and re-layouts  1.73 us (3%)
    pallas_call x1, Pallas kernels, body(): pl.pallas_call(functools.partial(exchange_kernel, n_blocks, count, float(...  58 us
    pallas_call x1, Pallas kernels, body(): pl.pallas_call(functools.partial(newton_kernel, count), out_shape=jax.Sha...  4.8 us
    unnamed x6, local copies, waits for them, and re-layouts  1.73 us

profile of v2, /device:TPU:56, one launch (start us, length us, event | category | flops | bytes accessed | tf_op | source)
XLA Modules:
  0.0 64.6 jit_solution(2130192307705592323)
XLA Ops:
  0.0 0.0 copy-start
  0.0 58.0 %exchange.1 = (bf16[16,2,64,128]{3,2,1,0:T(8,128)(2,1)}, f32[16,128]{1,0:T(8,128)}) custom-call(s32[7]{0:T(128)} %bitcast.3, bf16[1,7,512,512]{3,2,1,0:T(8,128)(2,1)} %grads_ref.1), custom_call_target="tpu_custom_call" | custom-call | flops 1879048192 | bytes 3670016 | tf_op jit(solution)/shard_map/exchange/pallas_call | solution.py:361
  58.0 0.0 copy-done
  58.0 0.0 copy-start.1
  58.0 1.0 %copy-done.1 = bf16[16,2,64,128]{3,2,1,0:T(8,128)(2,1)S(1)} copy-done((bf16[16,2,64,128]{3,2,1,0:T(8,128)(2,1)S(1)}, bf16[16,2,64,128]{3,2,1,0:T(8,128)(2,1)}, u32[]{:S(2)}) %copy-start.1) | copy-done | bytes 524312
  59.1 0.0 copy-start.2
  59.1 0.7 %copy-done.2 = f32[16,128]{1,0:T(8,128)S(1)} copy-done((f32[16,128]{1,0:T(8,128)S(1)}, f32[16,128]{1,0:T(8,128)}, u32[]{:S(2)}) %copy-start.2) | copy-done | bytes 8216
  59.8 4.8 %newton.1 = bf16[2,512,512]{2,1,0:T(8,128)(2,1)} custom-call(s32[7]{0:T(128)S(1)} %bitcast.4, s32[1]{0:T(128)} %bitcast.1.index_ref, bf16[16,2,64,128]{3,2,1,0:T(8,128)(2,1)S(1)} %copy-done.1, f32[16,128]{1,0:T(8,128)S(1)} %copy-done.2), custom_call_target="tpu_custom_call" | custom-call | flops 2147483648 | bytes 1048576 | tf_op jit(solution)/shard_map/newton/pallas_call | solution.py:396
Async XLA Ops:
  0.0 58.0 %copy-start = (s32[7,1]{0,1:T(1,128)S(1)}, s32[7,1]{0,1:T(1,128)}, u32[]{:S(2)}) copy-start(s32[7,1]{0,1:T(1,128)} %param.3) | copy-start | bytes 88
  58.0 1.0 %copy-start.1 = (bf16[16,2,64,128]{3,2,1,0:T(8,128)(2,1)S(1)}, bf16[16,2,64,128]{3,2,1,0:T(8,128)(2,1)}, u32[]{:S(2)}) copy-start(bf16[16,2,64,128]{3,2,1,0:T(8,128)(2,1)} %get-tuple-element.7.pieces_ref) | copy-start | bytes 1572868
  59.1 0.7 %copy-start.2 = (f32[16,128]{1,0:T(8,128)S(1)}, f32[16,128]{1,0:T(8,128)}, u32[]{:S(2)}) copy-start(f32[16,128]{1,0:T(8,128)} %get-tuple-element.8.diag_ref) | copy-start | bytes 24580

commit v3 on v2

v3 whole, which is shorter than its diff:
```python
import functools

import jax
import jax.numpy as jnp
from jax import lax
from jax.experimental import pallas as pl
from jax.experimental.pallas import tpu as pltpu
from jax.sharding import PartitionSpec as P

CAP = 2
CLIP = 0.25
RIDGE = 0.02
T = 128
QUARTER = 256
PIECE = 64
NX = 4
NY = 4
NC = 4
Y_FIRST = 2
EARLY = 4
MESH = pl.DeviceIdType.MESH
F32 = jnp.float32
BF16 = jnp.bfloat16


def gram(left, right):
    return lax.dot_general(left, right, (((1,), (1,)), ((), ())), preferred_element_type=F32)


def product(left, right):
    return lax.dot_general(left, right, (((1,), (0,)), ((), ())), preferred_element_type=F32)


def exchange_kernel(
    n_blocks, count, entries,
    owner_hbm, grads_ref, out_ref,
    g_buf, packed, first_x, first_y, sum_x, sum_y, second_x, second_y, stat, a2a_send, pieces, mat, roots,
    zbuf, cbuf, wbuf, ebuf, eybuf, owner_ref, slot_idx,
    g_sem, sems,
):
    nz = n_blocks // NC
    order = g_buf.shape[-1]
    n_y = min(Y_FIRST, count - 1)
    n_x = count - n_y
    me = lax.axis_index("dp")
    col = lax.axis_index("blocks")
    x, y = me // NY, me % NY
    z, c = col // NC, col % NC

    def device(xx, yy, zz, cc):
        return {"dp": xx * NY + yy, "blocks": zz * NC + cc}

    def x_peer(k):
        return lax.rem(x + k, NX)

    def y_peer(k):
        return lax.rem(y + k, NY)

    def c_peer(k):
        return lax.rem(c + k, NC)

    Z, C, X1, Y1, X2, Y2, E1, E2, OWN, A2A = range(10)

    def send(group, src, dst, dev):
        pltpu.make_async_remote_copy(
            src_ref=src, dst_ref=dst, send_sem=sems.at[0, group], recv_sem=sems.at[1, group],
            device_id=dev, device_id_type=MESH,
        ).start()

    def whole(group, like):
        return pltpu.make_async_remote_copy(
            src_ref=like, dst_ref=like, send_sem=sems.at[0, group], recv_sem=sems.at[1, group],
            device_id=device(x_peer(1), y, z, c), device_id_type=MESH,
        )

    def load(j):
        return pltpu.make_async_copy(grads_ref.at[0, j], g_buf.at[j], g_sem.at[j])

    barrier = pltpu.get_barrier_semaphore()

    def greet(dev):
        pl.semaphore_signal(barrier, inc=1, device_id=dev, device_id_type=MESH)

    def z_peers(act):
        if nz > 1:
            @pl.loop(1, nz)
            def _(k):
                act(lax.rem(z + k, nz))

    def plane_peers(act):
        @pl.loop(1, NX * NY)
        def _(k):
            act(lax.rem(me + k, NX * NY))

    def weight_peers(act, own_c):
        @pl.loop(0 if own_c else 1, NC)
        def _(k):
            @pl.loop(1, NX)
            def _(i):
                act(device(x_peer(i), y, z, c_peer(k)), 0)
                act(device(x, y_peer(i), z, c_peer(k)), 1)

        @pl.loop(1, NC)
        def _(k):
            act(device(x, y, z, c_peer(k)), 0)

    z_peers(lambda p: greet(device(x, y, p, c)))
    for j in range(count):
        load(j).start()
    owners = pltpu.make_async_copy(owner_hbm, owner_ref, sems.at[1, OWN])
    owners.start()
    weight_peers(lambda dev, axis: greet(dev), False)
    plane_peers(lambda p: greet({"dp": p, "blocks": col}))

    mine_x, mine_y = x * NC + c, (NX + y) * NC + c
    cbuf[mine_x] = jnp.zeros((8, T), F32)

    @pl.loop(0, count)
    def _(j):
        load(j).wait()
        values = g_buf[j].astype(F32)
        squares = jnp.sum((values * values).reshape(order // 8, 8, order), axis=0)
        part = squares[:, :T]
        for k in range(T, order, T):
            part = part + squares[:, k:k + T]
        cbuf[mine_x] += part

    rows = lax.broadcasted_iota(jnp.int32, (T, T), 0)
    cols = lax.broadcasted_iota(jnp.int32, (T, T), 1)
    lower = rows >= cols
    eye = rows == cols
    ebuf[x] = jnp.zeros((16, T), F32)

    def outer(j):
        top, bottom = g_buf[j, :256], g_buf[j, 256:]
        cross = gram(bottom, top)
        for t, (r, k) in enumerate(((0, 0), (0, 1), (1, 0), (1, 1))):
            packed[j, t // 2, (t % 2) * T:(t % 2 + 1) * T, :] = cross[
                r * T:(r + 1) * T, k * T:(k + 1) * T
            ].astype(BF16)
        for h, part in enumerate((top, bottom)):
            own = gram(part, part)
            d0, d1 = own[:T, :T], own[T:, T:]
            packed[j, 2, h * T:(h + 1) * T, :] = own[T:, :T].astype(BF16)
            packed[j, 3, h * T:(h + 1) * T, :] = jnp.where(lower, d0, d1).astype(BF16)
            ebuf[x, pl.ds(2 * j + h, 1), :] = jnp.sum(jnp.where(eye, d1, 0.0), axis=0, keepdims=True)

    def first_sends(j):
        @pl.when(j >= n_y)
        def _():
            @pl.loop(1, NX)
            def _(k):
                to = x_peer(k)
                send(X1, packed.at[j, to], first_x.at[x, j - n_y], device(to, y, z, c))

        if n_y:
            @pl.when(j < n_y)
            def _():
                @pl.loop(1, NY)
                def _(k):
                    to = y_peer(k)
                    send(Y1, packed.at[j, to], first_y.at[y, j], device(x, to, z, c))

    early = min(EARLY, count)
    pl.loop(0, early)(outer)

    pl.semaphore_wait(barrier, NX * NY - 1 + nz - 1 + (NX + NY - 1) * (NC - 1))

    def send_sum(dev, axis):
        send(C, cbuf.at[mine_x], cbuf.at[mine_x if axis == 0 else mine_y], dev)

    weight_peers(send_sum, True)
    c_like = cbuf.at[pl.ds(0, NX * NC - 1 + (NY - 1) * NC)]

    pl.loop(0, early)(first_sends)

    @pl.loop(early, count)
    def _(j):
        outer(j)
        first_sends(j)

    @pl.loop(1, NX)
    def _(k):
        send(E1, ebuf.at[x], ebuf.at[x], device(x_peer(k), y, z, c))

    whole(C, c_like).wait_recv()
    cbuf[mine_y] = cbuf[mine_x]
    sums = [jnp.sum(jnp.sum(cbuf[k * NC:(k + 1) * NC], axis=0), axis=0, keepdims=True) for k in range(NX + NY)]
    zbuf[z] = jnp.concatenate(sums, axis=0)
    z_peers(lambda p: send(Z, zbuf.at[z], zbuf.at[z], device(x, y, p, c)))

    owners.wait()

    @pl.loop(0, NX * NY * CAP)
    def _(i):
        target, slot = i // CAP, i % CAP
        found = jnp.int32(count)
        seen = jnp.int32(0)
        for j in range(count):
            hit = owner_ref[j] == target
            found = jnp.where(jnp.logical_and(hit, seen == slot), j, found)
            seen = seen + jnp.where(hit, 1, 0)
        slot_idx[i] = found

    stat[count] = jnp.zeros((PIECE, T), BF16)

    if nz > 1:
        whole(Z, zbuf.at[pl.ds(0, nz - 1)]).wait_recv()
    sums = jnp.sum(jnp.sum(zbuf[...], axis=0), axis=1, keepdims=True)
    scale = jnp.minimum(1.0, CLIP * lax.rsqrt(jnp.broadcast_to(sums, (NX + NY, T)) / entries + 1e-06))
    wbuf[...] = scale * scale / (NX * NY * order)

    def weight_x(k):
        return wbuf[pl.ds(k, 1), :]

    def weight_y(k):
        return wbuf[pl.ds(NX + k, 1), :]

    def wide(value):
        return value.astype(F32)

    whole(X1, first_x.at[pl.ds(0, NX - 1)]).wait_recv()

    @pl.loop(0, n_x)
    def _(j):
        got = weight_x(x) * wide(packed[n_y + j, x])
        for k in range(1, NX):
            got = got + weight_x(x_peer(k)) * wide(first_x[x_peer(k), j])
        sum_x[j] = got.astype(BF16)

    for k in range(1, NY):
        to = y_peer(k)
        piece = pl.ds(pl.multiple_of(to * PIECE, PIECE), PIECE)
        send(X2, sum_x.at[:, piece], second_x.at[y], device(x, to, z, c))

    if n_y:
        whole(Y1, first_y.at[pl.ds(0, NY - 1)]).wait_recv()

        @pl.loop(0, n_y)
        def _(j):
            got = weight_x(x) * wide(packed[j, y])
            for k in range(1, NY):
                got = got + weight_y(y_peer(k)) * wide(first_y[y_peer(k), j])
            sum_y[j] = got.astype(BF16)

        for k in range(1, NX):
            to = x_peer(k)
            piece = pl.ds(pl.multiple_of(to * PIECE, PIECE), PIECE)
            send(Y2, sum_y.at[:, piece], second_y.at[x], device(to, y, z, c))

    whole(E1, ebuf.at[pl.ds(0, NX - 1)]).wait_recv()
    diag = jnp.zeros((16, T), F32)
    for k in range(NX):
        diag = diag + wbuf[k:k + 1, :] * ebuf[k]
    eybuf[y] = diag

    @pl.loop(1, NY)
    def _(k):
        send(E2, eybuf.at[y], eybuf.at[y], device(x, y_peer(k), z, c))

    lane = lax.broadcasted_iota(jnp.int32, (PIECE, T), 1)
    row = lax.broadcasted_iota(jnp.int32, (PIECE, T), 0)

    def ridge(position):
        packed_row = position * PIECE + row
        on_diagonal = jnp.logical_and(packed_row >= 6 * T, packed_row % T == lane)
        return jnp.where(on_diagonal, RIDGE, 0.0).astype(F32)

    if n_y:
        whole(Y2, second_y.at[pl.ds(0, NX - 1)]).wait_recv()
        ridge_y = ridge(y * NX + x)

        @pl.loop(0, n_y)
        def _(j):
            got = wide(sum_y[j, pl.ds(pl.multiple_of(x * PIECE, PIECE), PIECE), :])
            for k in range(1, NX):
                got = got + wide(second_y[x_peer(k), j])
            stat[j] = (got + ridge_y).astype(BF16)

    whole(X2, second_x.at[pl.ds(0, NY - 1)]).wait_recv()
    ridge_x = ridge(x * NY + y)

    @pl.loop(0, n_x)
    def _(j):
        got = wide(sum_x[j, pl.ds(pl.multiple_of(y * PIECE, PIECE), PIECE), :])
        for k in range(1, NY):
            got = got + wide(second_x[y_peer(k), j])
        stat[n_y + j] = (got + ridge_x).astype(BF16)

    @pl.loop(0, CAP)
    def _(s):
        @pl.loop(1, NX * NY)
        def _(k):
            o = lax.rem(me + k, NX * NY)
            a2a_send[s, o] = stat[slot_idx[o * CAP + s]]
            send(A2A + s, a2a_send.at[s, o], pieces.at[s, me], {"dp": o, "blocks": col})

        pieces[s, me] = stat[slot_idx[me * CAP + s]]

    whole(E2, eybuf.at[pl.ds(0, NY - 1)]).wait_recv()
    diagonal = eybuf[0] + eybuf[1] + eybuf[2] + eybuf[3] + RIDGE
    diagonal_row = lax.broadcasted_iota(jnp.int32, (16, T), 0)
    unit5 = jnp.where(
        lax.broadcasted_iota(jnp.int32, (order, order), 0) == lax.broadcasted_iota(jnp.int32, (order, order), 1), 5.0, 0.0
    ).astype(F32)

    @pl.loop(0, CAP)
    def _(s):
        block = slot_idx[me * CAP + s]
        x_first = block >= n_y
        whole(A2A + s, a2a_send.at[0, pl.ds(0, NX * NY - 1)]).wait_recv()

        def tile(t):
            halves = []
            for p in (2 * t, 2 * t + 1):
                halves.append(jnp.where(x_first, wide(pieces[s, p]), wide(pieces[s, p % NX * NY + p // NX])))
            return jnp.concatenate(halves, axis=0)

        def put(r, k, value):
            mat[r * T:(r + 1) * T, k * T:(k + 1) * T] = value

        for t, (r, k) in enumerate(((2, 0), (2, 1), (3, 0), (3, 1), (1, 0), (3, 2))):
            value = tile(t)
            put(r, k, value)
            put(k, r, value.T)
        for h in range(2):
            value = tile(6 + h)
            turned = value.T
            edge = jnp.sum(jnp.where(diagonal_row == 2 * block + h, diagonal, 0.0), axis=0, keepdims=True)
            edge = wide(edge.astype(BF16))
            put(2 * h, 2 * h, jnp.where(lower, value, turned))
            put(2 * h + 1, 2 * h + 1, jnp.where(rows < cols, value, jnp.where(eye, edge, turned)))
        full = mat[...]
        z0 = 0.5 * order**0.5 * lax.rsqrt(jnp.sum(full * full, axis=(0, 1), keepdims=True) + 1e-06)
        coupled = z0 * full
        factor = ((unit5 - coupled) * 0.25).astype(BF16)
        iterate = (jnp.sqrt(jnp.sqrt(z0)) * wide(factor)).astype(BF16)
        square = product(factor, factor).astype(BF16)
        fourth = product(square, square).astype(BF16)
        coupled = product(fourth, coupled.astype(BF16))
        factor = ((unit5 - coupled) * 0.25).astype(BF16)
        root = product(iterate, factor)
        roots[s] = jnp.where(block < count, root, 0.0).astype(BF16)
        pltpu.make_async_copy(roots.at[s], out_ref.at[s], sems.at[0, OWN]).start()

    if nz > 1:
        whole(Z, zbuf.at[pl.ds(0, nz - 1)]).wait_send()
    whole(C, c_like).wait_send()
    whole(X1, first_x.at[pl.ds(0, NX - 1)]).wait_send()
    whole(X2, second_x.at[pl.ds(0, NY - 1)]).wait_send()
    if n_y:
        whole(Y1, first_y.at[pl.ds(0, NY - 1)]).wait_send()
        whole(Y2, second_y.at[pl.ds(0, NX - 1)]).wait_send()
    whole(E1, ebuf.at[pl.ds(0, NX - 1)]).wait_send()
    whole(E2, eybuf.at[pl.ds(0, NY - 1)]).wait_send()
    for s in range(CAP):
        whole(A2A + s, a2a_send.at[0, pl.ds(0, NX * NY - 1)]).wait_send()
    pltpu.make_async_copy(roots, out_ref, sems.at[0, OWN]).wait()


def finish_kernel(roots_ref, out_ref, sem):
    copy = pltpu.make_async_copy(roots_ref, out_ref, sem)
    copy.start()
    copy.wait()


def body(n_blocks, grads, owner):
    count, order = grads.shape[1], grads.shape[2]
    entries = n_blocks * count * order * order
    n = NX * NY
    n_y = min(Y_FIRST, count - 1)
    n_x = count - n_y
    nz = n_blocks // NC
    dma = pltpu.SemaphoreType.DMA
    vmem = pltpu.VMEM
    roots = pl.pallas_call(
        functools.partial(exchange_kernel, n_blocks, count, float(entries)),
        out_shape=jax.ShapeDtypeStruct((CAP, order, order), BF16),
        in_specs=[pl.BlockSpec(memory_space=pl.ANY), pl.BlockSpec(memory_space=pl.ANY)],
        out_specs=pl.BlockSpec(memory_space=pl.ANY),
        scratch_shapes=[
            vmem((count, order, order), BF16),
            vmem((count, NX, QUARTER, T), BF16),
            vmem((NX, n_x, QUARTER, T), BF16),
            vmem((NY, max(n_y, 1), QUARTER, T), BF16),
            vmem((n_x, QUARTER, T), BF16),
            vmem((max(n_y, 1), QUARTER, T), BF16),
            vmem((NY, n_x, PIECE, T), BF16),
            vmem((NX, max(n_y, 1), PIECE, T), BF16),
            vmem((count + 1, PIECE, T), BF16),
            vmem((CAP, n, PIECE, T), BF16),
            vmem((CAP, n, PIECE, T), BF16),
            vmem((order, order), F32),
            vmem((CAP, order, order), BF16),
            vmem((nz, 8, T), F32),
            vmem(((NX + NY) * NC, 8, T), F32),
            vmem((NX + NY, T), F32),
            vmem((NX, 16, T), F32),
            vmem((NY, 16, T), F32),
            pltpu.SMEM((count,), jnp.int32),
            pltpu.SMEM((n * CAP,), jnp.int32),
            dma((count,)),
            dma((2, 9 + CAP)),
        ],
        compiler_params=pltpu.CompilerParams(
            collective_id=0, has_side_effects=True, vmem_limit_bytes=61 * 1024 * 1024
        ),
        cost_estimate=pl.CostEstimate(
            flops=2 * count * order**3 + 16 * order**3, bytes_accessed=grads.size * 2, transcendentals=0
        ),
        name="exchange",
    )(owner[:, 0], grads)
    out = pl.pallas_call(
        finish_kernel,
        out_shape=jax.ShapeDtypeStruct((CAP, order, order), BF16),
        in_specs=[pl.BlockSpec(memory_space=pl.ANY)],
        out_specs=pl.BlockSpec(memory_space=pl.ANY),
        scratch_shapes=[dma(())],
        cost_estimate=pl.CostEstimate(flops=0, bytes_accessed=4 * CAP * order * order, transcendentals=0),
        compiler_params=pltpu.CompilerParams(vmem_limit_bytes=63 * 1024 * 1024),
        name="finish",
    )(roots)
    return out[None, None]


def solution(mesh):
    return jax.shard_map(
        functools.partial(body, mesh.shape["blocks"]),
        mesh=mesh,
        in_specs=(P("dp", "blocks", None, None), P("blocks", None)),
        out_specs=P("blocks", "dp", None, None, None),
        check_vma=False,
    )
```

time: 64.8 us -> 91.4 us (1.41)
  Pallas kernels: 62.8 us -> 91.3 us
  local copies, waits for them, and re-layouts: 1.73 us -> 0 us
    pallas_call x1, Pallas kernels: 4.8 us -> 32.9 us  [body(): pl.pallas_call(finish_kernel, out_shape=jax.ShapeDtypeStruct((CAP, order,...]
    unnamed x6 -> x0, local copies, waits for them, and re-layouts: 1.73 us -> none
where the time goes in v3:
time: 91.4 us; the launch traced here: 91.3 us
  Pallas kernels  91.3 us (100%)
    pallas_call x1, Pallas kernels, body(): pl.pallas_call(functools.partial(exchange_kernel, n_blocks, count, float(...  58.4 us
    pallas_call x1, Pallas kernels, body(): pl.pallas_call(finish_kernel, out_shape=jax.ShapeDtypeStruct((CAP, order,...  32.9 us

profile of v3, /device:TPU:56, one launch (start us, length us, event | category | flops | bytes accessed | tf_op | source)
XLA Modules:
  0.0 91.3 jit_solution(14540699461854190054)
XLA Ops:
  0.0 58.4 %exchange.1.roots_ref = bf16[2,512,512]{2,1,0:T(8,128)(2,1)} custom-call(s32[7]{0:T(128)} %bitcast.2, bf16[1,7,512,512]{3,2,1,0:T(8,128)(2,1)} %grads_ref.1), custom_call_target="tpu_custom_call" | custom-call | flops 4026531840 | bytes 3670016 | tf_op jit(solution)/shard_map/exchange/pallas_call | solution.py:376
  58.4 32.9 %finish.1 = bf16[2,512,512]{2,1,0:T(8,128)(2,1)} custom-call(bf16[2,512,512]{2,1,0:T(8,128)(2,1)} %exchange.1.roots_ref), custom_call_target="tpu_custom_call" | custom-call | bytes 2097152 | tf_op jit(solution)/shard_map/finish/pallas_call | solution.py:413

commit v4 on v3

--- a/solution.py
+++ b/solution.py
@@ -356,12 +356,6 @@
     for s in range(CAP):
         whole(A2A + s, a2a_send.at[0, pl.ds(0, NX * NY - 1)]).wait_send()
     pltpu.make_async_copy(roots, out_ref, sems.at[0, OWN]).wait()
-
-
-def finish_kernel(roots_ref, out_ref, sem):
-    copy = pltpu.make_async_copy(roots_ref, out_ref, sem)
-    copy.start()
-    copy.wait()
 
 
 def body(n_blocks, grads, owner):
@@ -410,17 +404,7 @@
         ),
         name="exchange",
     )(owner[:, 0], grads)
-    out = pl.pallas_call(
-        finish_kernel,
-        out_shape=jax.ShapeDtypeStruct((CAP, order, order), BF16),
-        in_specs=[pl.BlockSpec(memory_space=pl.ANY)],
-        out_specs=pl.BlockSpec(memory_space=pl.ANY),
-        scratch_shapes=[dma(())],
-        cost_estimate=pl.CostEstimate(flops=0, bytes_accessed=4 * CAP * order * order, transcendentals=0),
-        compiler_params=pltpu.CompilerParams(vmem_limit_bytes=63 * 1024 * 1024),
-        name="finish",
-    )(roots)
-    return out[None, None]
+    return roots[None, None]
 
 
 def solution(mesh):

time: 91.4 us -> 60.9 us (0.67)
  Pallas kernels: 91.3 us -> 58.4 us
  local copies, waits for them, and re-layouts: 0 us -> 2.26 us
    pallas_call x1 -> x0, Pallas kernels: 32.9 us -> none  [body(): pl.pallas_call(finish_kernel, out_shape=jax.ShapeDtypeStruct((CAP, order,...]
    unnamed x0 -> x1, local copies, waits for them, and re-layouts: none -> 2.26 us
where the time goes in v4:
time: 60.9 us; the launch traced here: 60.7 us
  Pallas kernels  58.4 us (96%)
  local copies, waits for them, and re-layouts  2.26 us (4%)
    pallas_call x1, Pallas kernels, body(): pl.pallas_call(functools.partial(exchange_kernel, n_blocks, count, float(...  58.4 us
    unnamed x1, local copies, waits for them, and re-layouts  2.26 us

profile of v4, /device:TPU:56, one launch (start us, length us, event | category | flops | bytes accessed | tf_op | source)
XLA Modules:
  0.0 60.7 jit_solution(16681961637739079091)
XLA Ops:
  0.0 58.4 %exchange.1 = bf16[2,512,512]{2,1,0:T(8,128)(2,1)} custom-call(s32[7]{0:T(128)} %bitcast.3, bf16[1,7,512,512]{3,2,1,0:T(8,128)(2,1)} %grads_ref.1), custom_call_target="tpu_custom_call" | custom-call | flops 4026531840 | bytes 3670016 | tf_op jit(solution)/shard_map/exchange/pallas_call | solution.py:370
  58.4 2.3 %copy.4 = bf16[1,1,2,512,512]{4,3,2,1,0:T(8,128)(2,1)} copy(bf16[1,1,2,512,512]{4,3,2,1,0:T(8,128)(2,1)} %bitcast.2) | data formatting | bytes 2097152

commit v5 on v4

--- a/solution.py
+++ b/solution.py
@@ -82,10 +82,8 @@
         pl.semaphore_signal(barrier, inc=1, device_id=dev, device_id_type=MESH)
 
     def z_peers(act):
-        if nz > 1:
-            @pl.loop(1, nz)
-            def _(k):
-                act(lax.rem(z + k, nz))
+        for k in range(1, nz):
+            act(lax.rem(z + k, nz))
 
     def plane_peers(act):
         @pl.loop(1, NX * NY)
@@ -93,15 +91,11 @@
             act(lax.rem(me + k, NX * NY))
 
     def weight_peers(act, own_c):
-        @pl.loop(0 if own_c else 1, NC)
-        def _(k):
-            @pl.loop(1, NX)
-            def _(i):
+        for k in range(1, NC + 1 if own_c else NC):
+            for i in range(1, NX):
                 act(device(x_peer(i), y, z, c_peer(k)), 0)
                 act(device(x, y_peer(i), z, c_peer(k)), 1)
-
-        @pl.loop(1, NC)
-        def _(k):
+        for k in range(1, NC):
             act(device(x, y, z, c_peer(k)), 0)
 
     z_peers(lambda p: greet(device(x, y, p, c)))
@@ -221,7 +215,7 @@
 
     whole(X1, first_x.at[pl.ds(0, NX - 1)]).wait_recv()
 
-    @pl.loop(0, n_x)
+    @pl.loop(0, n_x, unroll=n_x)
     def _(j):
         got = weight_x(x) * wide(packed[n_y + j, x])
         for k in range(1, NX):
@@ -236,7 +230,7 @@
     if n_y:
         whole(Y1, first_y.at[pl.ds(0, NY - 1)]).wait_recv()
 
-        @pl.loop(0, n_y)
+        @pl.loop(0, n_y, unroll=n_y)
         def _(j):
             got = weight_x(x) * wide(packed[j, y])
             for k in range(1, NY):
@@ -270,7 +264,7 @@
         whole(Y2, second_y.at[pl.ds(0, NX - 1)]).wait_recv()
         ridge_y = ridge(y * NX + x)
 
-        @pl.loop(0, n_y)
+        @pl.loop(0, n_y, unroll=n_y)
         def _(j):
             got = wide(sum_y[j, pl.ds(pl.multiple_of(x * PIECE, PIECE), PIECE), :])
             for k in range(1, NX):
@@ -280,7 +274,7 @@
     whole(X2, second_x.at[pl.ds(0, NY - 1)]).wait_recv()
     ridge_x = ridge(x * NY + y)
 
-    @pl.loop(0, n_x)
+    @pl.loop(0, n_x, unroll=n_x)
     def _(j):
         got = wide(sum_x[j, pl.ds(pl.multiple_of(y * PIECE, PIECE), PIECE), :])
         for k in range(1, NY):
@@ -289,7 +283,7 @@
 
     @pl.loop(0, CAP)
     def _(s):
-        @pl.loop(1, NX * NY)
+        @pl.loop(1, NX * NY, unroll=5)
         def _(k):
             o = lax.rem(me + k, NX * NY)
             a2a_send[s, o] = stat[slot_idx[o * CAP + s]]

time: 60.9 us -> 60.7 us (level)
  no operation moved by 1% of the time
where the time goes in v5:
time: 60.7 us; the launch traced here: 60.5 us
  Pallas kernels  58.3 us (96%)
  local copies, waits for them, and re-layouts  2.26 us (4%)
    pallas_call x1, Pallas kernels, body(): pl.pallas_call(functools.partial(exchange_kernel, n_blocks, count, float(...  58.3 us
    unnamed x1, local copies, waits for them, and re-layouts  2.26 us

profile of v5, /device:TPU:56, one launch (start us, length us, event | category | flops | bytes accessed | tf_op | source)
XLA Modules:
  0.0 60.5 jit_solution(7031884250921499775)
XLA Ops:
  0.0 58.3 %exchange.1 = bf16[2,512,512]{2,1,0:T(8,128)(2,1)} custom-call(s32[7]{0:T(128)} %bitcast.3, bf16[1,7,512,512]{3,2,1,0:T(8,128)(2,1)} %grads_ref.1), custom_call_target="tpu_custom_call" | custom-call | flops 4026531840 | bytes 3670016 | tf_op jit(solution)/shard_map/exchange/pallas_call | solution.py:364
  58.3 2.3 %copy.4 = bf16[1,1,2,512,512]{4,3,2,1,0:T(8,128)(2,1)} copy(bf16[1,1,2,512,512]{4,3,2,1,0:T(8,128)(2,1)} %bitcast.2) | data formatting | bytes 2097152
